TPU v7x, 512 devices: a whole 4x8x8 slice. The times are simulated.
512 devices in a mesh: section: 4 (over y_lo), expert: 128 (over y_hi, x, z, core).
Axes of the slice: x: 4, y: 8 (y_hi: 2, y_lo: 4; y = y_hi * 4 + y_lo), z: 8, core: 2. Of those that a mesh axis runs over, the one named last changes fastest.
Arguments:
- enc_states: bfloat16 [4, 16384, 2080], P('section', 'expert'), may hold values from -6 to 6
- patch_start: int32 [128], P('expert'), may hold values from 0 to 120
- patch_layer: int32 [128], P('expert'), may hold values from 1 to 3
- enc_gain: float32 [2080], replicated, may hold values from 0.1 to 1.9
- dec_states: bfloat16 [4, 2048, 2080], P('section', 'expert'), may hold values from -6 to 6
- queries: bfloat16 [4, 2048, 1024], P('section', 'expert'), may hold values from -1.796875 to 1.796875
- attn_weight: bfloat16 [4, 3, 2080, 1024], P('section', None, None, 'expert'), may hold values from -0.125 to 0.125
- ffn_gain: float32 [4, 2080], P('section'), may hold values from 0.1 to 1.9
- expert_in: bfloat16 [4, 128, 2080, 384], P('section', 'expert'), may hold values from -0.125 to 0.125
- expert_out: bfloat16 [4, 128, 384, 2080], P('section', 'expert'), may hold values from -0.109375 to 0.109375
- expert_id: int32 [4, 2048, 1], P('section', 'expert'), may hold values from 0 to 15; in each aligned block of 16 rows (0 to 15, 16 to 31, ..., all dimensions but the last counted through in order) at most 2 rows name the same one
- gate: float32 [4, 2048], P('section', 'expert'), may hold values from 0.3 to 1
Outputs:
- layer_out: bfloat16 [4, 2048, 2080], P('section', 'expert')
- memory: bfloat16 [16384, 2080], P('expert')
Inputs may be any that keep to these rules, and one draw needn't show every extreme that they name: `expert_id`: within the 16 rows of one device of each section no expert is named more than 2 times, and some device's rows name one expert exactly 2 times.
All inputs are finite; a program needn't handle non-finite values.
Results may differ from a plain program's by a relative error of at most 0.017.
Values may be sent and summed in bfloat16 or wider, within the bound.
A program may use at most 128 MiB of HBM per device.

v0:
```python
import jax
import jax.numpy as jnp
from jax import lax
from jax.sharding import PartitionSpec as P

HEAD_DIM = 64
HEADS = 16
PATCH = 8


def spread(array, axis, root):
    mine = lax.axis_index(axis) == root
    return lax.psum(jnp.where(mine, array, jnp.zeros_like(array)), axis)


def rms_norm(values, gain):
    return values * lax.rsqrt(jnp.mean(values * values, axis=-1, keepdims=True) + 1e-06) * gain


def per_device(
    enc_states,
    patch_start,
    patch_layer,
    enc_gain,
    dec_states,
    queries,
    attn_weight,
    ffn_gain,
    expert_in,
    expert_out,
    expert_id,
    gate,
):
    section_index = lax.axis_index("section")
    own_block = enc_states[0]
    source_len, width = own_block.shape
    window_start = patch_start[0]
    layer_pick = patch_layer[0]
    clean_rows = lax.dynamic_slice_in_dim(own_block, window_start, PATCH, 0)
    chosen = jnp.where(layer_pick == section_index, 1.0, 0.0).astype(jnp.float32)
    restored = lax.psum((clean_rows.astype(jnp.float32) * chosen).astype(jnp.bfloat16), "section")
    patched = lax.dynamic_update_slice_in_dim(own_block, restored, window_start, 0)
    local_memory = rms_norm(patched.astype(jnp.float32), enc_gain).astype(jnp.bfloat16)
    memory = spread(local_memory, "section", 0)
    weights = lax.all_gather(attn_weight[0], "expert", axis=2, tiled=True)
    decoder_rows = dec_states[0]
    target_len = decoder_rows.shape[0]
    inner_width = weights.shape[2]
    query_matrix_rows = queries[0].reshape(target_len, HEADS, HEAD_DIM)
    key_matrix_rows = jnp.dot(memory, weights[0], preferred_element_type=jnp.float32).reshape(
        source_len, HEADS, HEAD_DIM
    )
    logit_scores = jnp.einsum(
        "pvx,evx->vpe", query_matrix_rows.astype(jnp.float32), key_matrix_rows
    )
    value_matrix_rows = jnp.dot(memory, weights[1], preferred_element_type=jnp.float32).reshape(
        source_len, HEADS, HEAD_DIM
    )
    exponent = jnp.exp(logit_scores)
    device_portions = exponent / jnp.sum(exponent, axis=-1, keepdims=True)
    context = (
        jnp.einsum("ign,nis->gis", device_portions, value_matrix_rows)
        .reshape(target_len, inner_width)
        .astype(jnp.bfloat16)
    )
    attended = lax.dot_general(
        context, weights[2], (((1,), (1,)), ((), ())), preferred_element_type=jnp.float32
    )
    residual = (decoder_rows.astype(jnp.float32) + attended).astype(jnp.bfloat16)
    normed = rms_norm(residual.astype(jnp.float32), ffn_gain[0]).astype(jnp.bfloat16)
    device_list = lax.axis_size("expert")
    split_parts = min(8, device_list // 2)
    experts = device_list // split_parts
    capacity = min(target_len, max(2, 2 * target_len // experts))
    expert_ids = expert_id[0, :, 0]
    expert_range = jnp.arange(experts, dtype=jnp.int32)
    slot_range = jnp.arange(capacity, dtype=jnp.int32)
    member = (expert_ids[:, None] == expert_range[None, :]).astype(jnp.int32)
    earlier = jnp.cumsum(member, axis=0)
    slot_index = jnp.sum(member * earlier, axis=1) - 1
    select_map = (
        (expert_ids[None, None, :] == expert_range[:, None, None])
        & (slot_index[None, None, :] == slot_range[None, :, None])
    ).astype(jnp.bfloat16)
    dispatch = jnp.einsum(
        "ect,td->ecd", select_map, normed, preferred_element_type=jnp.float32
    ).astype(jnp.bfloat16)
    outgoing = jnp.broadcast_to(dispatch[:, None], (experts, split_parts, capacity, width)).reshape(
        device_list, capacity, width
    )
    w_in = expert_in[0, 0]
    w_out = expert_out[0, 0]
    arrived = lax.all_to_all(outgoing, "expert", split_axis=0, concat_axis=0, tiled=True)
    token_rows = arrived.reshape(-1, width)
    hidden = jax.nn.relu(jnp.dot(token_rows, w_in, preferred_element_type=jnp.float32)).astype(
        jnp.bfloat16
    )
    partial_value = (
        jnp.dot(hidden, w_out, preferred_element_type=jnp.float32)
        .astype(jnp.bfloat16)
        .reshape(arrived.shape)
    )
    returned_rows = lax.all_to_all(partial_value, "expert", split_axis=0, concat_axis=0, tiled=True)
    combined = jnp.sum(
        returned_rows.reshape(experts, split_parts, capacity, width).astype(jnp.float32), axis=1
    )
    expert_sum = jnp.einsum("ect,ecd->td", select_map.astype(jnp.float32), combined)
    layer_out = (residual.astype(jnp.float32) + gate[0][:, None] * expert_sum).astype(jnp.bfloat16)
    return (layer_out[None], memory)


def solution(mesh):
    in_specs = (
        P("section", "expert", None),
        P("expert"),
        P("expert"),
        P(),
        P("section", "expert", None),
        P("section", "expert", None),
        P("section", None, None, "expert"),
        P("section", None),
        P("section", "expert", None, None),
        P("section", "expert", None, None),
        P("section", "expert", None),
        P("section", "expert"),
    )
    out_specs = (P("section", "expert", None), P("expert", None))
    return jax.shard_map(
        per_device, mesh=mesh, in_specs=in_specs, out_specs=out_specs, check_vma=False
    )
```

profile of v0, /device:TPU:1, one launch (start us, length us, event | category | flops | bytes accessed | tf_op | source)
XLA Modules:
  0.0 314.5 jit_solution(1263474027698655858)
XLA Ops:
  8.0 0.0 all-gather.3.cloned.1.call-start
  8.1 1.2 copy.38
  9.2 0.0 all-gather.3.cloned.1.call-update
  9.2 0.0 all-reduce.2.cloned.1.call-start
  10.6 0.2 fusion.40
  10.8 26.0 %psum.14 = bf16[8,2080]{0,1:T(8,128)(2,1)S(1)} all-reduce(bf16[8,2080]{0,1:T(8,128)(2,1)S(1)} %fusion.40), channel_id=1, replica_groups=mesh['section'=4,'expert'=128] {'section'}, use_global_device_ids=true, to_apply=%region_0.1 | all-reduce | flops 16640 | bytes 66560 | tf_op jit(solution)/shard_map/psum | solution.py:41
  36.9 4.6 %dynamic_update_slice.3 = bf16[128,2080]{0,1:T(8,128)(2,1)S(1)} dynamic-update-slice(bf16[128,2080]{0,1:T(8,128)(2,1)S(1)} %bitcast.84, bf16[8,2080]{0,1:T(8,128)(2,1)S(1)} %psum.14, s32[]{:T(128)S(6)} %select_n.17, s32[]{:T(128)} %constant.12.clone.1) | dynamic-update-slice | bytes 66564 | tf_op jit(solution)/shard_map/dynamic_update_slice | solution.py:42
  41.4 0.3 fusion.37
  41.7 1.1 fusion.41
  42.9 0.0 all-reduce.2.cloned.1.call-update
  42.9 0.1 fusion.58
  43.0 0.1 iota_compare_fusion.1
  43.1 0.1 reshape_squeeze.3
  43.2 0.2 select_reduce_fusion
  43.5 150.3 %all-gather.3.cloned.1.call-done = bf16[1,3,2080,1024]{2,3,1,0:T(8,128)(2,1)} async-done(((bf16[1,3,2080,8]{2,3,1,0:T(8,128)(2,1)}), bf16[1,3,2080,1024]{2,3,1,0:T(8,128)(2,1)}) %all-gather.3.cloned.1.call-update) | async-done | bytes 12779536 | tf_op jit(solution)/shard_map/all_gather | solution.py:45
  193.8 7.6 %fusion.65 = (bf16[1,1,2080,1024]{2,3,1,0:T(8,128)(2,1)}, bf16[1,1,2080,1024]{2,3,1,0:T(8,128)(2,1)}) fusion(bf16[1,3,2080,1024]{2,3,1,0:T(8,128)(2,1)} %all-gather.3.cloned.1.call-done), kind=kLoop, calls=%fused_computation.62 | loop fusion | bytes 17039360 | tf_op jit(solution)/shard_map/slice | solution.py:50
  201.4 4.0 %fusion.28 = f32[16,16,128]{2,1,0:T(8,128)S(1)} fusion(bf16[16,64,2080]{2,1,0:T(8,128)(2,1)} %bitcast.83, bf16[128,2080]{0,1:T(8,128)(2,1)} %all-reduce.2.cloned.1.call-done, bf16[16,16,64]{2,1,0:T(8,128)(2,1)S(1)} %reshape_squeeze.3), kind=kOutput, calls=%fused_computation.25 | convolution fusion | flops 549453824 | bytes 4956160 | tf_op jit(solution)/shard_map/pvx,evx->vpe/dot_general | solution.py:53
  205.4 3.9 %fusion.34 = bf16[16,16,64]{2,0,1:T(8,128)(2,1)S(1)} fusion(bf16[16,64,2080]{2,1,0:T(8,128)(2,1)} %bitcast.82, bf16[128,2080]{0,1:T(8,128)(2,1)S(1)} %copy-done.1, f32[16,16,128]{2,1,0:T(8,128)S(1)} %fusion.28), kind=kOutput, calls=%fused_computation.27 | convolution fusion | flops 549503360 | bytes 4956160 | tf_op jit(solution)/shard_map/ign,nis->gis/dot_general | solution.py:62
  209.3 0.1 convert_element_type.74
  209.4 3.1 multiply_reduce_fusion
  212.5 0.3 convolution_convert_fusion.1
  212.8 0.1 copy.25
  212.9 0.6 broadcast_in_dim.7
  213.5 39.6 %all_to_all.10 = bf16[128,2,2080]{2,1,0:T(2,128)(2,1)S(1)} all-to-all(bf16[128,2,2080]{2,1,0:T(2,128)(2,1)S(1)} %bitcast.85), channel_id=1, replica_groups=mesh['section'=4,'expert'=128] {'expert'}, dimensions={0} | all-to-all | bytes 2129920 | tf_op jit(solution)/shard_map/all_to_all | solution.py:93
  253.1 1.7 reshape.102
  254.7 4.2 %convolution_convert_fusion = bf16[256,2080]{0,1:T(8,128)(2,1)} fusion(bf16[1,1,384,2080]{2,3,1,0:T(8,128)(2,1)S(1)} %copy-done, bf16[256,2080]{1,0:T(8,128)(2,1)} %reshape.102, bf16[1,1,2080,384]{3,2,1,0:T(8,128)(2,1)} %param.20), kind=kOutput, calls=%fused_computation.2 | convolution fusion | flops 818618368 | bytes 5324800 | tf_op jit(solution)/shard_map/dot_general | solution.py:99
  259.0 1.6 copy.26
  260.6 1.3 reshape.103
  261.9 42.5 %all_to_all.11 = bf16[128,2,2080]{2,1,0:T(2,128)(2,1)S(1)} all-to-all(bf16[128,2,2080]{2,1,0:T(2,128)(2,1)} %reshape.103), channel_id=1, replica_groups=mesh['section'=4,'expert'=128] {'expert'}, dimensions={0} | all-to-all | bytes 2129920 | tf_op jit(solution)/shard_map/all_to_all | solution.py:103
  304.4 1.0 convert_reduce_fusion
  305.3 0.9 fusion.7
  306.3 0.8 copy.39
  (24 shorter events, 0.2 us)
Async XLA Ops:
  8.0 246.7 %copy-start = (bf16[1,1,384,2080]{2,3,1,0:T(8,128)(2,1)S(1)}, bf16[1,1,384,2080]{2,3,1,0:T(8,128)(2,1)}, u32[]{:S(2)}) copy-start(bf16[1,1,384,2080]{2,3,1,0:T(8,128)(2,1)} %param.21) | copy-start | bytes 4792324
  8.0 185.8 %all-gather.3.cloned.1.call-start = ((), (), s32[]{:S(2)}) async-start(), calls=%async_computation.3 | async-start | bytes 13473792 | tf_op jit(solution)/shard_map/all_gather | solution.py:45
  9.2 192.1 %all-reduce.2.cloned.1.call-start = ((), (), s32[]{:S(2)}) async-start(), calls=%async_computation.2 | async-start | bytes 1064960 | tf_op jit(solution)/shard_map/psum | solution.py:13
  10.8 30.9 %copy-start.4 = (f32[2080]{0:T(1024)S(1)}, f32[2080]{0:T(1024)}, u32[]{:S(2)}) copy-start(f32[2080]{0:T(1024)} %param.15) | copy-start | bytes 24964
  36.8 6.1 %copy-start.6 = (s32[1,16,1]{1,2,0:T(1,128)S(1)}, s32[1,16,1]{1,2,0:T(1,128)}, u32[]{:S(2)}) copy-start(s32[1,16,1]{1,2,0:T(1,128)} %param.22) | copy-start | bytes 196
  36.8 6.2 %copy-start.3 = (bf16[1,16,1024]{2,1,0:T(8,128)(2,1)S(1)}, bf16[1,16,1024]{2,1,0:T(8,128)(2,1)}, u32[]{:S(2)}) copy-start(bf16[1,16,1024]{2,1,0:T(8,128)(2,1)} %param.17) | copy-start | bytes 98308
  36.8 6.6 %copy-start.5 = (f32[1,2080]{1,0:T(1,128)S(1)}, f32[1,2080]{1,0:T(1,128)}, u32[]{:S(2)}) copy-start(f32[1,2080]{1,0:T(1,128)} %param.19) | copy-start | bytes 24964
  201.4 4.0 %copy-start.1 = (bf16[128,2080]{0,1:T(8,128)(2,1)S(1)}, bf16[128,2080]{0,1:T(8,128)(2,1)}, u32[]{:S(2)}) copy-start(bf16[128,2080]{0,1:T(8,128)(2,1)} %all-reduce.2.cloned.1.call-done) | copy-start | bytes 1597444
  205.4 4.0 %copy-start.2 = (bf16[1,16,2080]{2,1,0:T(8,128)(2,1)S(1)}, bf16[1,16,2080]{2,1,0:T(8,128)(2,1)}, u32[]{:S(2)}) copy-start(bf16[1,16,2080]{2,1,0:T(8,128)(2,1)} %param.16) | copy-start | bytes 199684
  261.9 43.4 %copy-start.7 = (f32[1,16]{1,0:T(1,128)S(1)}, f32[1,16]{1,0:T(1,128)}, u32[]{:S(2)}) copy-start(f32[1,16]{1,0:T(1,128)} %param.23) | copy-start | bytes 196
Sparse Core Ops, SparseCore 0:
  13.3 180.3 all-gather.2
Sparse Core Ops, SparseCore 1:
  43.0 70.9 all-reduce.1
where the time goes:
time: 317 us; the launch traced here: 315 us
  waiting for transfers between devices  150 us (47%)
  blocking collectives  108 us (34%)
  local copies, waits for them, and re-layouts  19.6 us (6%)
  between operations  17 us (5%)
  matrix products  16.3 us (5%)
    all_gather x1, waiting for transfers between devices, per_device(): weights = lax.all_gather(attn_weight[0], 'expert', axis=2, tiled=True)  150 us
    all_to_all x1, blocking collectives, per_device(): lax.all_to_all(partial_value, 'expert', split_axis=0, concat_axis=0, tile...  42.5 us
    all_to_all x1, blocking collectives, per_device(): lax.all_to_all(outgoing, 'expert', split_axis=0, concat_axis=0, tiled=True)  39.6 us
    psum x1, blocking collectives, per_device(): lax.psum((clean_rows.astype(jnp.float32) * chosen).astype(jnp.bfloat16),...  26 us
    slice x1, local copies, waits for them, and re-layouts, per_device(): weights[0]  7.59 us
  transfers between devices with their start and end apart: 2, of which 1 were waited for; matrix products, arithmetic and copies ran while one was open for 5% of the time, Pallas kernels for 0%

commit v1 on v0

v1 whole, which is shorter than its diff:
```python
import jax
import jax.numpy as jnp
from jax import lax
from jax.experimental import pallas as pl
from jax.experimental.pallas import tpu as pltpu
from jax.sharding import PartitionSpec as P

HEAD_DIM = 64
PATCH = 8
CHUNK = 16
EPS = 1e-06
BF, F32 = jnp.bfloat16, jnp.float32
NT = (((1,), (1,)), ((), ()))
NN = (((1,), (0,)), ((), ()))


def dot(a, b, dims=NN):
    return lax.dot_general(a, b, dims, preferred_element_type=F32)


def kernel(
    start_ref, layer_ref, enc_ref, enc_gain_ref, dec_ref, q_ref, w_ref, ffn_gain_ref,
    w_in_ref, w_out_ref, id_row_ref, id_col_ref, gate_ref,
    out_ref, memory_ref,
    raw, win, mem, w0, wz, qg, part, pr, ds, dbuf, d1, g, y, rb, rz, rt, d2, ret, w_in, w_out,
    load_sem, wx_s, wx_r, raw_s, raw_r, win_s, win_r, q_s, q_r, self_sem,
    xr_s, xr_r, xl_s, xl_r, x2_s, x2_r, sib_s, sib_r, zr_s, zr_r, zl_s, zl_r,
    p_s, p_r, d1_s, d1_r, g_s, g_r, gs_s, gs_r, rb_s, rb_r, rz_s, rz_r, d2_s, d2_r,
):
    s = lax.axis_index("section")
    e = lax.axis_index("expert")
    c = lax.rem(e, 2)
    z = lax.rem(e // 2, 8)
    x = lax.rem(e // 16, 4)
    yh = e // 64
    zh, zl = z // 4, lax.rem(z, 4)

    def at(yy, xx, zz, cc, ss=None):
        return (s if ss is None else ss, ((yy * 4 + xx) * 8 + zz) * 2 + cc)

    def mod(v, n):
        return lax.rem(v + n, n)

    sibling = at(yh, x, z, 1 - c)
    right, left = at(yh, mod(x + 1, 4), z, c), at(yh, mod(x - 1, 4), z, c)
    up, down = at(yh, x, mod(z + 1, 8), c), at(yh, x, mod(z - 1, 8), c)
    me8 = x * 2 + c
    me16 = yh * 8 + x * 2 + zh
    role = [(dx, dc) for dx in range(4) for dc in range(2)]

    def role_of(dx, dc):
        xx = mod(x + dx, 4)
        cc = lax.rem(c + dc, 2)
        return xx, cc

    def expert_of(i):
        yy = lax.rem(yh + i // 8, 2)
        xx = mod(x + (i // 2) % 4, 4)
        if i % 2:
            zz_h, zz_l = 1 - zh, 3 - zl
        else:
            zz_h, zz_l = zh, zl
        return yy * 8 + xx * 2 + zz_h, at(yy, xx, zz_h * 4 + zz_l, c)

    pending = []

    def copy(src, dst, ssem, rsem, dev):
        return pltpu.make_async_remote_copy(
            src_ref=src, dst_ref=dst, send_sem=ssem, recv_sem=rsem, device_id=dev,
            device_id_type=pl.DeviceIdType.MESH,
        )

    def send(src, dst, ssem, rsem, dev):
        d = copy(src, dst, ssem, rsem, dev)
        d.start()
        pending.append(d)

    def arrived(dst, rsem):
        copy(dst, dst, rsem, rsem, sibling).wait_recv()

    loads = [
        pltpu.make_async_copy(w_in_ref, w_in, load_sem.at[0]),
        pltpu.make_async_copy(w_out_ref, w_out, load_sem.at[1]),
    ]
    for d in loads:
        d.start()

    barrier = pltpu.get_barrier_semaphore()
    peers = [at(yh, x, z, c, lax.rem(s + k, 4)) for k in (1, 2, 3)]
    peers += [at(yh, *role_of(dx, dc)[:1], z, role_of(dx, dc)[1]) for dx, dc in role[1:]]
    peers += [up, down]
    peers += [at(1 - yh, x, z, cc) for cc in (0, 1)]
    peers += [at(yh, x, zh * 4 + lax.rem(zl + k, 4), c) for k in (1, 2, 3)]
    peers += [expert_of(i)[1] for i in range(1, 16)]
    for dev in peers:
        pl.semaphore_signal(barrier, inc=1, device_id=dev, device_id_type=pl.DeviceIdType.MESH)

    start = start_ref[0]
    layer = layer_ref[0]

    @pl.when(s == 0)
    def _():
        raw[...] = enc_ref[...]

    @pl.when(s > 0)
    def _():
        row = lax.broadcasted_iota(jnp.int32, (16, 128), 0)
        col = lax.broadcasted_iota(jnp.int32, (16, 128), 1)
        pick = ((col == row + start) & (row < PATCH)).astype(F32).astype(BF)
        block = enc_ref[...].reshape(128, enc_ref.shape[-1])
        win[s - 1] = dot(pick, block).astype(BF)

    pl.semaphore_wait(barrier, len(peers))

    for yy in (0, 1):
        here = (yh == yy) & (c == yh)

        @pl.when(here)
        def _(yy=yy):
            pltpu.make_async_copy(w_ref, w0.at[c], self_sem.at[0]).start()

        @pl.when(jnp.logical_not(here))
        def _(yy=yy):
            copy(w_ref, w0.at[c], wx_s.at[yy], wx_r.at[c], at(yy, x, z, yh)).start()

    @pl.when(s == 0)
    def _():
        for k in range(8):
            copy(raw.at[k], raw.at[k], raw_s.at[k], raw_r.at[k], at(yh, x, z, c, 1)).start()

    @pl.when(s > 0)
    def _():
        for k in (1, 2, 3):
            copy(
                win.at[s - 1], win.at[s - 1], win_s.at[k - 1], win_r.at[s - 1],
                at(yh, x, z, c, lax.rem(s + k, 4)),
            ).start()

    for i, (dx, dc) in enumerate(role):
        xx, cc = role_of(dx, dc)
        cols = pl.ds(pl.multiple_of((cc * 4 + xx) * 128, 128), 128)
        if i == 0:
            qg[me8] = q_ref[:, cols]
        else:
            send(q_ref.at[:, cols], qg.at[me8], q_s.at[i], q_r.at[i], at(yh, xx, z, cc))

    def patched_chunk(k):
        @pl.when(s > 0)
        def _():
            arrived(raw.at[k], raw_r.at[k])

        @pl.when((s > 0) & (s < 3))
        def _():
            copy(raw.at[k], raw.at[k], raw_s.at[k], raw_r.at[k], at(yh, x, z, c, s + 1)).start()

        if k == 0:
            for i in range(3):
                @pl.when(s != i + 1)
                def _(i=i):
                    arrived(win.at[i], win_r.at[i])

        row = lax.broadcasted_iota(jnp.int32, (CHUNK, 16), 0) + k * CHUNK - start
        slot = lax.broadcasted_iota(jnp.int32, (CHUNK, 16), 1)
        pick = ((row == slot) & (slot < PATCH)).astype(F32).astype(BF)
        window = jnp.where(layer == 1, win[0], jnp.where(layer == 2, win[1], win[2]))
        fresh = dot(pick, window)
        at_row = lax.broadcasted_iota(jnp.int32, fresh.shape, 0) + k * CHUNK - start
        values = jnp.where((at_row >= 0) & (at_row < PATCH), fresh, raw[k].astype(F32))
        scale = lax.rsqrt(jnp.mean(values * values, axis=-1, keepdims=True) + EPS)
        normed = (values * scale * enc_gain_ref[...]).astype(BF)
        mem[me8, k] = normed
        memory_ref[k] = normed
        send(mem.at[me8, k], mem.at[me8, k], xr_s.at[k], xr_r.at[k], right)
        send(mem.at[me8, k], mem.at[me8, k], xl_s.at[k], xl_r.at[k], left)
        send(mem.at[me8, k], mem.at[me8, k], sib_s.at[0, k], sib_r.at[0, k], sibling)

    q_left, q_right, q_far = (mod(x + d, 4) * 2 + c for d in (3, 1, 2))

    def neighbour_chunk(k):
        arrived(mem.at[q_left, k], xr_r.at[k])
        block = mem.at[q_left, k]
        if k < 4:
            send(block, block, x2_s.at[k], x2_r.at[k], right)
        send(block, block, sib_s.at[3, k], sib_r.at[3, k], sibling)
        arrived(mem.at[q_right, k], xl_r.at[k])
        block = mem.at[q_right, k]
        if k >= 4:
            send(block, block, x2_s.at[k], x2_r.at[k], left)
        send(block, block, sib_s.at[1, k], sib_r.at[1, k], sibling)

    def far_chunk(k):
        block = mem.at[q_far, k]
        arrived(block, x2_r.at[k])
        send(block, block, sib_s.at[2, k], sib_r.at[2, k], sibling)

    def own_weights():
        for cc in (0, 1):
            here = (c == yh) & (c == cc)

            @pl.when(here)
            def _(cc=cc):
                pltpu.make_async_copy(w_ref, w0.at[cc], self_sem.at[0]).wait()

            @pl.when(jnp.logical_not(here))
            def _(cc=cc):
                arrived(w0.at[cc], wx_r.at[cc])

        for m in range(3):
            both = jnp.concatenate([w0[0, m].astype(F32), w0[1, m].astype(F32)], axis=0)
            wz[m, z] = both.astype(BF)
        ring_step(1)

    def ring_blocks(r):
        if r < 4:
            return pl.ds(0, 3), pl.ds(0, 3)
        return pl.ds(0, 2), pl.ds(2, 1)

    def ring_step(r):
        ms_up, ms_down = ring_blocks(r)
        block = wz.at[ms_up, mod(z - (r - 1), 8)]
        send(block, block, zr_s.at[r - 1], zr_r.at[r - 1], up)
        block = wz.at[ms_down, mod(z + (r - 1), 8)]
        send(block, block, zl_s.at[r - 1], zl_r.at[r - 1], down)

    def ring_arrived(r):
        ms_up, ms_down = ring_blocks(r)
        arrived(wz.at[ms_up, mod(z - r, 8)], zr_r.at[r - 1])
        arrived(wz.at[ms_down, mod(z + r, 8)], zl_r.at[r - 1])
        if r < 4:
            ring_step(r + 1)

    A, B, C, Z = patched_chunk, neighbour_chunk, far_chunk, ring_arrived
    A(0), A(1), own_weights(), A(2), A(3), B(0), Z(1), A(4), B(1), A(5), B(2), A(6), Z(2), B(3)
    A(7), B(4), B(5), Z(3), B(6), B(7), C(0), C(1), C(2), C(3), Z(4), C(4), C(5), C(6), C(7)
    for dx in range(4):
        q = mod(x + dx, 4) * 2 + (1 - c)
        for k in range(8):
            arrived(mem.at[q, k], sib_r.at[dx, k])
    for i, (dx, dc) in enumerate(role[1:], 1):
        arrived(qg.at[mod(x - dx, 4) * 2 + lax.rem(c + dc, 2)], q_r.at[i])

    width = enc_ref.shape[-1]
    first_head = lax.broadcasted_iota(jnp.int32, (16, 128), 1) < HEAD_DIM

    def attend(q, carry):
        rows = mem[q].reshape(128, width)
        kv = dot(rows, wz[0:2].reshape(256, width), NT)
        keys, values = kv[:, :128].astype(BF), kv[:, 128:].astype(BF)
        ask = qg[q].astype(F32)
        ask = jnp.concatenate([jnp.where(first_head, ask, 0.0), jnp.where(first_head, 0.0, ask)], axis=0)
        exponent = jnp.exp(dot(ask.astype(BF), keys, NT))
        shares = exponent / jnp.sum(exponent, axis=-1, keepdims=True)
        mixed = dot(shares.astype(BF), values)
        context = jnp.where(first_head, mixed[:16], mixed[16:]).astype(BF)
        part[q] = dot(context, wz[2].reshape(128, width)).astype(BF)
        return carry

    lax.fori_loop(0, 8, attend, 0)

    for i, (dx, dc) in enumerate(role[1:], 1):
        xx, cc = role_of(dx, dc)
        send(part.at[xx * 2 + cc], pr.at[me8], p_s.at[i], p_r.at[i], at(yh, xx, z, cc))
    total = dec_ref[...].astype(F32) + part[me8].astype(F32)
    for i, (dx, dc) in enumerate(role[1:], 1):
        q = mod(x - dx, 4) * 2 + lax.rem(c + dc, 2)
        arrived(pr.at[q], p_r.at[i])
        total = total + pr[q].astype(F32)
    residual = total.astype(BF)
    total = residual.astype(F32)
    scale = lax.rsqrt(jnp.mean(total * total, axis=-1, keepdims=True) + EPS)
    normed = (total * scale * ffn_gain_ref[...]).astype(BF)

    row = lax.broadcasted_iota(jnp.int32, (16, 16), 0)
    col = lax.broadcasted_iota(jnp.int32, (16, 16), 1)
    id_row, id_col = id_row_ref[...], id_col_ref[...]
    same = (jnp.broadcast_to(id_row, (16, 16)) == jnp.broadcast_to(id_col, (16, 16))).astype(F32)
    slot_row = jnp.sum(jnp.where(row < col, same, 0.0), axis=0, keepdims=True)
    slot_col = jnp.sum(jnp.where(col < row, same, 0.0), axis=1, keepdims=True)
    number = lax.broadcasted_iota(jnp.int32, (32, 16), 0)
    chosen = (lax.rem(number, 16) == id_row) & ((number // 16).astype(F32) == slot_row)
    picked = dot(chosen.astype(F32).astype(BF), normed)
    ds[:, 0, :] = picked[:16]
    ds[:, 1, :] = picked[16:]
    dbuf[...] = ds[...].astype(BF)

    for i in range(1, 16):
        block, dev = expert_of(i)
        send(dbuf.at[block], d1.at[me16], d1_s.at[i], d1_r.at[i], dev)
    d1[me16] = dbuf[me16]

    def back(i):
        yy = lax.rem(yh + i // 8, 2)
        xx = mod(x - (i // 2) % 4, 4)
        return yy * 8 + xx * 2 + (1 - zh if i % 2 else zh)

    for i in range(1, 16):
        arrived(d1.at[back(i)], d1_r.at[i])
    ds[...] = d1[...].astype(F32)
    g[zl, c] = jnp.concatenate([ds[:, 0, :], ds[:, 1, :]], axis=0).astype(BF)

    block = g.at[zl, c]
    for k in (1, 2, 3):
        send(block, block, g_s.at[k], g_r.at[k], at(yh, x, zh * 4 + lax.rem(zl + k, 4), c))
    send(block, block, gs_s.at[0], gs_r.at[0], sibling)
    for d in loads:
        d.wait()
    for k in (1, 2, 3):
        block = g.at[mod(zl - k, 4), c]
        arrived(block, g_r.at[k])
        send(block, block, gs_s.at[k], gs_r.at[k], sibling)
    for k in range(4):
        arrived(g.at[mod(zl - k, 4), 1 - c], gs_r.at[k])

    hidden = jnp.maximum(dot(g[...].reshape(256, width), w_in[...]), 0.0).astype(BF)
    y[...] = dot(hidden, w_out[...], NT).astype(BF).reshape(y.shape)

    order = (1, 2, 3, 0)
    for k in order:
        to = lax.rem(zl + k, 4)
        send(y.at[to, 1 - c], rb.at[to], rb_s.at[k], rb_r.at[k], sibling)
    for k in order:
        to = lax.rem(zl + k, 4)
        arrived(rb.at[to], rb_r.at[k])
        pair = y[to, c].astype(F32) + rb[to].astype(F32)
        if k:
            rt[to] = pair.astype(BF)
            send(rt.at[to], rz.at[zl], rz_s.at[k], rz_r.at[k], at(yh, x, zh * 4 + to, c))
        else:
            total = pair
    for k in (1, 2, 3):
        src = mod(zl - k, 4)
        arrived(rz.at[src], rz_r.at[k])
        total = total + rz[src].astype(F32)
    ds[:, 0, :] = total[:16]
    ds[:, 1, :] = total[16:]
    d2[...] = ds[...].astype(BF)
    for i in range(1, 16):
        block, dev = expert_of(i)
        send(d2.at[block], ret.at[me16], d2_s.at[i], d2_r.at[i], dev)
    ret[me16] = d2[me16]
    for i in range(1, 16):
        arrived(ret.at[back(i)], d2_r.at[i])
    ds[...] = ret[...].astype(F32)
    slots = jnp.concatenate([ds[:, 0, :], ds[:, 1, :]], axis=0).astype(BF)
    number = lax.broadcasted_iota(jnp.int32, (16, 32), 1)
    chosen = (lax.rem(number, 16) == id_col) & ((number // 16).astype(F32) == slot_col)
    combined = dot(chosen.astype(F32).astype(BF), slots)
    out_ref[...] = (residual.astype(F32) + gate_ref[...] * combined).astype(BF)

    for d in pending:
        d.wait_send()
    for yy in (0, 1):
        @pl.when(jnp.logical_not((yh == yy) & (c == yh)))
        def _(yy=yy):
            copy(w_ref, w0.at[c], wx_s.at[yy], wx_r.at[c], at(yy, x, z, yh)).wait_send()

    @pl.when(s < 3)
    def _():
        for k in range(8):
            copy(raw.at[k], raw.at[k], raw_s.at[k], raw_r.at[k], sibling).wait_send()

    @pl.when(s > 0)
    def _():
        for k in (1, 2, 3):
            copy(
                win.at[s - 1], win.at[s - 1], win_s.at[k - 1], win_r.at[s - 1], sibling
            ).wait_send()


def per_device(
    enc_states, patch_start, patch_layer, enc_gain, dec_states, queries, attn_weight, ffn_gain,
    expert_in, expert_out, expert_id, gate,
):
    rows, width = enc_states.shape[1:]
    hid = expert_in.shape[-1]
    dma = lambda *shape: pltpu.SemaphoreType.DMA(shape)
    vm = lambda *shape: pltpu.VMEM(shape, BF)
    vmem = pl.BlockSpec(memory_space=pltpu.VMEM)
    smem = pl.BlockSpec(memory_space=pltpu.SMEM)
    hbm = pl.BlockSpec(memory_space=pl.ANY)
    scratch = [
        vm(8, 16, width), vm(3, 16, width), vm(8, 8, 16, width), vm(2, 3, 8, width),
        vm(3, 8, 16, width), vm(8, 16, 128), vm(8, 16, width), vm(8, 16, width),
        pltpu.VMEM((16, 2, width), F32), vm(16, 2, width), vm(16, 2, width),
        vm(4, 2, 32, width), vm(4, 2, 32, width), vm(4, 32, width), vm(4, 32, width),
        vm(4, 32, width), vm(16, 2, width), vm(16, 2, width), vm(width, hid), vm(width, hid),
        dma(2), dma(2), dma(2), dma(8), dma(8), dma(3), dma(3), dma(8), dma(8), dma(1),
        dma(8), dma(8), dma(8), dma(8), dma(8), dma(8), dma(4, 8), dma(4, 8),
        dma(4), dma(4), dma(4), dma(4),
        dma(8), dma(8), dma(16), dma(16), dma(4), dma(4), dma(4), dma(4), dma(4), dma(4),
        dma(4), dma(4), dma(16), dma(16),
    ]
    out, memory = pl.pallas_call(
        kernel,
        out_shape=(
            jax.ShapeDtypeStruct(dec_states.shape[1:], BF),
            jax.ShapeDtypeStruct((8, 16, width), BF),
        ),
        in_specs=[smem, smem] + [vmem] * 6 + [hbm, hbm] + [vmem] * 3,
        out_specs=(vmem, vmem),
        scratch_shapes=scratch,
        compiler_params=pltpu.CompilerParams(
            collective_id=0, has_side_effects=True, vmem_limit_bytes=50 * 1024 * 1024
        ),
    )(
        patch_start, patch_layer, enc_states[0].reshape(8, 16, width), enc_gain.reshape(1, width),
        dec_states[0], queries[0], jnp.transpose(attn_weight[0], (0, 2, 1)), ffn_gain,
        expert_in[0, 0], expert_out[0, 0].T, expert_id[0].reshape(1, 16), expert_id[0],
        gate.reshape(16, 1),
    )
    return out[None], memory.reshape(rows, width)


def solution(mesh):
    in_specs = (
        P("section", "expert", None),
        P("expert"),
        P("expert"),
        P(),
        P("section", "expert", None),
        P("section", "expert", None),
        P("section", None, None, "expert"),
        P("section", None),
        P("section", "expert", None, None),
        P("section", "expert", None, None),
        P("section", "expert", None),
        P("section", "expert"),
    )
    out_specs = (P("section", "expert", None), P("expert", None))
    return jax.shard_map(
        per_device, mesh=mesh, in_specs=in_specs, out_specs=out_specs, check_vma=False
    )
```

time: 317 us -> 142 us (0.45)
  the two profiles are of different devices: /device:TPU:1 before, /device:TPU:24 now
where the time goes in v1:
time: 142 us; the launch traced here: 141 us
  Pallas kernels  129 us (91%)
  local copies, waits for them, and re-layouts  10.5 us (7%)
  between operations  1.95 us (1%)
    pallas_call x1, Pallas kernels, per_device(): pl.pallas_call(kernel, out_shape=(jax.ShapeDtypeStruct(dec_states.shape[1...  129 us
    unnamed x15, local copies, waits for them, and re-layouts  8.28 us

profile of v1, /device:TPU:24, one launch (start us, length us, event | category | flops | bytes accessed | tf_op | source)
XLA Modules:
  0.0 141.3 jit_solution(3351770907527970015)
XLA Ops:
  1.9 0.7 copy.16.gate_ref
  2.7 0.7 copy.15.id_col_ref
  3.4 0.7 reshape.13.enc_gain_ref
  4.1 1.3 copy.14
  5.4 0.0 copy-start
  5.4 1.4 copy-done
  6.9 0.0 copy-start.1
  6.9 0.9 copy-done.1
  7.7 0.0 copy-start.2
  7.8 0.9 copy-done.2
  8.6 0.0 copy-start.3
  8.6 0.8 copy-done.3
  9.4 0.0 copy-start.4
  9.4 0.7 copy-done.4
  10.1 0.0 copy-start.5
  10.1 0.7 copy-done.5
  10.7 128.9 %shard_map.131 = (bf16[16,2080]{1,0:T(8,128)(2,1)S(1)}, bf16[8,16,2080]{2,1,0:T(8,128)(2,1)S(1)}) custom-call(s32[1]{0:T(128)S(6)} %copy.19.start_ref, s32[1]{0:T(128)S(6)} %copy.20.layer_ref, bf16[8,16,2080]{2,1,0:T(8,128)(2,1)S(1)} %bitcast.15, f32[1,2080]{1,0:T(1,128)S(1)} %reshape.13.enc_gain_ref, bf16[16,2080]{1,0:T(8,128)(2,1)S(1)} %bitcast.19, ...), custom_call_target="tpu_custom_call" | custom-call | tf_op jit(solution)/shard_map/pallas_call | solution.py:393
  139.6 1.0 copy.17
  140.6 0.6 copy.21
Async XLA Ops:
  5.4 1.4 %copy-start = (bf16[1,1,2080,384]{3,2,1,0:T(8,128)(2,1)S(1)}, bf16[1,1,2080,384]{3,2,1,0:T(8,128)(2,1)}, u32[]{:S(2)}) copy-start(bf16[1,1,2080,384]{3,2,1,0:T(8,128)(2,1)} %param.20) | copy-start | bytes 4792324
  6.9 0.9 copy-start.1
  7.7 0.9 copy-start.2
  8.6 0.8 copy-start.3
  9.4 0.7 copy-start.4
  10.1 0.7 copy-start.5

commit v2 on v1

--- a/solution.py
+++ b/solution.py
@@ -19,14 +19,26 @@
 
 
 def kernel(
-    start_ref, layer_ref, enc_ref, enc_gain_ref, dec_ref, q_ref, w_ref, ffn_gain_ref,
-    w_in_ref, w_out_ref, id_row_ref, id_col_ref, gate_ref,
+    start_hbm, layer_hbm, enc_hbm, enc_gain_hbm, dec_hbm, q_hbm, w_hbm, ffn_gain_hbm,
+    w_in_hbm, w_out_hbm, id_hbm, gate_hbm,
     out_ref, memory_ref,
-    raw, win, mem, w0, wz, qg, part, pr, ds, dbuf, d1, g, y, rb, rz, rt, d2, ret, w_in, w_out,
+    start_ref, layer_ref, enc_ref, enc_gain_ref, dec_ref, q_ref, w_ref, ffn_gain_ref, w_in, w_out, id_ref, gate_ref,
+    raw, win, mem, w0, wz, qg, part, pr, ds, dbuf, d1, g, y, rb, rz, rt, d2, ret,
     load_sem, wx_s, wx_r, raw_s, raw_r, win_s, win_r, q_s, q_r, self_sem,
     xr_s, xr_r, xl_s, xl_r, x2_s, x2_r, sib_s, sib_r, zr_s, zr_r, zl_s, zl_r,
     p_s, p_r, d1_s, d1_r, g_s, g_r, gs_s, gs_r, rb_s, rb_r, rz_s, rz_r, d2_s, d2_r,
 ):
+    width = enc_ref.shape[0]
+
+    moves = [
+        (w_hbm, w_ref), (enc_hbm, enc_ref), (q_hbm, q_ref), (enc_gain_hbm, enc_gain_ref.at[0]),
+        (dec_hbm, dec_ref), (ffn_gain_hbm, ffn_gain_ref), (id_hbm, id_ref), (gate_hbm, gate_ref),
+        (w_in_hbm, w_in), (w_out_hbm, w_out), (start_hbm, start_ref), (layer_hbm, layer_ref),
+    ]
+    loads = [pltpu.make_async_copy(a, b, load_sem.at[i]) for i, (a, b) in enumerate(moves)]
+    for d in loads:
+        d.start()
+
     s = lax.axis_index("section")
     e = lax.axis_index("expert")
     c = lax.rem(e, 2)
@@ -77,13 +89,6 @@
 
     def arrived(dst, rsem):
         copy(dst, dst, rsem, rsem, sibling).wait_recv()
-
-    loads = [
-        pltpu.make_async_copy(w_in_ref, w_in, load_sem.at[0]),
-        pltpu.make_async_copy(w_out_ref, w_out, load_sem.at[1]),
-    ]
-    for d in loads:
-        d.start()
 
     barrier = pltpu.get_barrier_semaphore()
     peers = [at(yh, x, z, c, lax.rem(s + k, 4)) for k in (1, 2, 3)]
@@ -95,20 +100,26 @@
     for dev in peers:
         pl.semaphore_signal(barrier, inc=1, device_id=dev, device_id_type=pl.DeviceIdType.MESH)
 
+    loads[10].wait()
+    loads[11].wait()
     start = start_ref[0]
     layer = layer_ref[0]
+    loads[0].wait()
+    loads[1].wait()
 
     @pl.when(s == 0)
     def _():
-        raw[...] = enc_ref[...]
+        row = lax.broadcasted_iota(jnp.int32, (128, 128), 0)
+        col = lax.broadcasted_iota(jnp.int32, (128, 128), 1)
+        turn = (col == row).astype(F32).astype(BF)
+        raw[...] = dot(turn, enc_ref[...], NT).astype(BF).reshape(8, CHUNK, width)
 
     @pl.when(s > 0)
     def _():
         row = lax.broadcasted_iota(jnp.int32, (16, 128), 0)
         col = lax.broadcasted_iota(jnp.int32, (16, 128), 1)
         pick = ((col == row + start) & (row < PATCH)).astype(F32).astype(BF)
-        block = enc_ref[...].reshape(128, enc_ref.shape[-1])
-        win[s - 1] = dot(pick, block).astype(BF)
+        win[s - 1] = dot(pick, enc_ref[...], NT).astype(BF)
 
     pl.semaphore_wait(barrier, len(peers))
 
@@ -136,6 +147,8 @@
                 at(yh, x, z, c, lax.rem(s + k, 4)),
             ).start()
 
+    loads[2].wait()
+    loads[3].wait()
     for i, (dx, dc) in enumerate(role):
         xx, cc = role_of(dx, dc)
         cols = pl.ds(pl.multiple_of((cc * 4 + xx) * 128, 128), 128)
@@ -144,6 +157,11 @@
         else:
             send(q_ref.at[:, cols], qg.at[me8], q_s.at[i], q_r.at[i], at(yh, xx, z, cc))
 
+    q_left, q_right, q_far = (mod(x + d, 4) * 2 + c for d in (3, 1, 2))
+
+    def go(src, dst, ssem, rsem, dev):
+        copy(src, dst, ssem, rsem, dev).start()
+
     def patched_chunk(k):
         @pl.when(s > 0)
         def _():
@@ -151,47 +169,66 @@
 
         @pl.when((s > 0) & (s < 3))
         def _():
-            copy(raw.at[k], raw.at[k], raw_s.at[k], raw_r.at[k], at(yh, x, z, c, s + 1)).start()
-
-        if k == 0:
-            for i in range(3):
-                @pl.when(s != i + 1)
-                def _(i=i):
-                    arrived(win.at[i], win_r.at[i])
-
-        row = lax.broadcasted_iota(jnp.int32, (CHUNK, 16), 0) + k * CHUNK - start
+            go(raw.at[k], raw.at[k], raw_s.at[k], raw_r.at[k], at(yh, x, z, c, s + 1))
+
+        for i in range(3):
+            @pl.when((s != i + 1) & (k == 0))
+            def _(i=i):
+                arrived(win.at[i], win_r.at[i])
+
+        first = k * CHUNK - start
+        row = lax.broadcasted_iota(jnp.int32, (CHUNK, 16), 0) + first
         slot = lax.broadcasted_iota(jnp.int32, (CHUNK, 16), 1)
         pick = ((row == slot) & (slot < PATCH)).astype(F32).astype(BF)
         window = jnp.where(layer == 1, win[0], jnp.where(layer == 2, win[1], win[2]))
         fresh = dot(pick, window)
-        at_row = lax.broadcasted_iota(jnp.int32, fresh.shape, 0) + k * CHUNK - start
+        at_row = lax.broadcasted_iota(jnp.int32, fresh.shape, 0) + first
         values = jnp.where((at_row >= 0) & (at_row < PATCH), fresh, raw[k].astype(F32))
         scale = lax.rsqrt(jnp.mean(values * values, axis=-1, keepdims=True) + EPS)
         normed = (values * scale * enc_gain_ref[...]).astype(BF)
         mem[me8, k] = normed
         memory_ref[k] = normed
-        send(mem.at[me8, k], mem.at[me8, k], xr_s.at[k], xr_r.at[k], right)
-        send(mem.at[me8, k], mem.at[me8, k], xl_s.at[k], xl_r.at[k], left)
-        send(mem.at[me8, k], mem.at[me8, k], sib_s.at[0, k], sib_r.at[0, k], sibling)
-
-    q_left, q_right, q_far = (mod(x + d, 4) * 2 + c for d in (3, 1, 2))
+        block = mem.at[me8, k]
+        go(block, block, xr_s.at[k], xr_r.at[k], right)
+        go(block, block, xl_s.at[k], xl_r.at[k], left)
+        go(block, block, sib_s.at[0, k], sib_r.at[0, k], sibling)
 
     def neighbour_chunk(k):
-        arrived(mem.at[q_left, k], xr_r.at[k])
         block = mem.at[q_left, k]
-        if k < 4:
-            send(block, block, x2_s.at[k], x2_r.at[k], right)
-        send(block, block, sib_s.at[3, k], sib_r.at[3, k], sibling)
-        arrived(mem.at[q_right, k], xl_r.at[k])
-        block = mem.at[q_right, k]
-        if k >= 4:
-            send(block, block, x2_s.at[k], x2_r.at[k], left)
-        send(block, block, sib_s.at[1, k], sib_r.at[1, k], sibling)
+        arrived(block, xr_r.at[k])
+
+        @pl.when(k < 4)
+        def _():
+            go(block, block, x2_s.at[k], x2_r.at[k], right)
+
+        go(block, block, sib_s.at[3, k], sib_r.at[3, k], sibling)
+        other = mem.at[q_right, k]
+        arrived(other, xl_r.at[k])
+
+        @pl.when(k >= 4)
+        def _():
+            go(other, other, x2_s.at[k], x2_r.at[k], left)
+
+        go(other, other, sib_s.at[1, k], sib_r.at[1, k], sibling)
 
     def far_chunk(k):
         block = mem.at[q_far, k]
         arrived(block, x2_r.at[k])
-        send(block, block, sib_s.at[2, k], sib_r.at[2, k], sibling)
+        go(block, block, sib_s.at[2, k], sib_r.at[2, k], sibling)
+
+    def ring_up(r, m):
+        block = wz.at[m, mod(z - r + 8, 8)]
+        go(block, block, zr_s.at[r, m], zr_r.at[r, m], up)
+
+    def ring_down(r, m):
+        block = wz.at[m, mod(z + r, 8)]
+        go(block, block, zl_s.at[r, m], zl_r.at[r, m], down)
+
+    def from_down(r, m):
+        arrived(wz.at[m, mod(z - r + 7, 8)], zr_r.at[r, m])
+
+    def from_up(r, m):
+        arrived(wz.at[m, mod(z + r + 1, 8)], zl_r.at[r, m])
 
     def own_weights():
         for cc in (0, 1):
@@ -208,58 +245,87 @@
         for m in range(3):
             both = jnp.concatenate([w0[0, m].astype(F32), w0[1, m].astype(F32)], axis=0)
             wz[m, z] = both.astype(BF)
-        ring_step(1)
-
-    def ring_blocks(r):
-        if r < 4:
-            return pl.ds(0, 3), pl.ds(0, 3)
-        return pl.ds(0, 2), pl.ds(2, 1)
-
-    def ring_step(r):
-        ms_up, ms_down = ring_blocks(r)
-        block = wz.at[ms_up, mod(z - (r - 1), 8)]
-        send(block, block, zr_s.at[r - 1], zr_r.at[r - 1], up)
-        block = wz.at[ms_down, mod(z + (r - 1), 8)]
-        send(block, block, zl_s.at[r - 1], zl_r.at[r - 1], down)
-
-    def ring_arrived(r):
-        ms_up, ms_down = ring_blocks(r)
-        arrived(wz.at[ms_up, mod(z - r, 8)], zr_r.at[r - 1])
-        arrived(wz.at[ms_down, mod(z + r, 8)], zl_r.at[r - 1])
-        if r < 4:
-            ring_step(r + 1)
-
-    A, B, C, Z = patched_chunk, neighbour_chunk, far_chunk, ring_arrived
-    A(0), A(1), own_weights(), A(2), A(3), B(0), Z(1), A(4), B(1), A(5), B(2), A(6), Z(2), B(3)
-    A(7), B(4), B(5), Z(3), B(6), B(7), C(0), C(1), C(2), C(3), Z(4), C(4), C(5), C(6), C(7)
-    for dx in range(4):
-        q = mod(x + dx, 4) * 2 + (1 - c)
-        for k in range(8):
-            arrived(mem.at[q, k], sib_r.at[dx, k])
+            ring_up(0, m)
+            ring_down(0, m)
+
+    first_a = 2 * s
+    first_w, first_z = 3, 5
+
+    def tick(t, carry):
+        k = t - first_a
+
+        @pl.when((k >= 0) & (k < 8))
+        def _():
+            patched_chunk(k)
+
+        @pl.when(t == first_w)
+        def _():
+            own_weights()
+
+        kb = k - 3
+
+        @pl.when((kb >= 0) & (kb < 8))
+        def _():
+            neighbour_chunk(kb)
+
+        j = t - first_z
+        r, m = j // 3, lax.rem(j, 3)
+
+        @pl.when((j >= 0) & (j < 8))
+        def _():
+            from_down(r, m)
+            ring_up(r + 1, m)
+
+        @pl.when((j >= 0) & ((j < 6) | (j == 8)))
+        def _():
+            from_up(r, m)
+            ring_down(r + 1, m)
+
+        return carry
+
+    lax.fori_loop(0, 17, tick, 0)
+    from_down(2, 2), from_down(3, 0), from_down(3, 1)
+    from_up(2, 0), from_up(2, 1), from_up(3, 2)
     for i, (dx, dc) in enumerate(role[1:], 1):
         arrived(qg.at[mod(x - dx, 4) * 2 + lax.rem(c + dc, 2)], q_r.at[i])
 
-    width = enc_ref.shape[-1]
     first_head = lax.broadcasted_iota(jnp.int32, (16, 128), 1) < HEAD_DIM
 
-    def attend(q, carry):
-        rows = mem[q].reshape(128, width)
-        kv = dot(rows, wz[0:2].reshape(256, width), NT)
-        keys, values = kv[:, :128].astype(BF), kv[:, 128:].astype(BF)
-        ask = qg[q].astype(F32)
-        ask = jnp.concatenate([jnp.where(first_head, ask, 0.0), jnp.where(first_head, 0.0, ask)], axis=0)
-        exponent = jnp.exp(dot(ask.astype(BF), keys, NT))
-        shares = exponent / jnp.sum(exponent, axis=-1, keepdims=True)
-        mixed = dot(shares.astype(BF), values)
-        context = jnp.where(first_head, mixed[:16], mixed[16:]).astype(BF)
-        part[q] = dot(context, wz[2].reshape(128, width)).astype(BF)
-        return carry
-
-    lax.fori_loop(0, 8, attend, 0)
-
-    for i, (dx, dc) in enumerate(role[1:], 1):
-        xx, cc = role_of(dx, dc)
-        send(part.at[xx * 2 + cc], pr.at[me8], p_s.at[i], p_r.at[i], at(yh, xx, z, cc))
+    def attend(dx):
+        xx = mod(x + dx, 4)
+        for k in range(8):
+            arrived(mem.at[xx * 2 + (1 - c), k], sib_r.at[dx, k])
+        rows = mem[pl.ds(xx * 2, 2)].reshape(256, width)
+        kv = dot(rows, wz[0:2].reshape(256, width), NT).astype(BF)
+        for cc in (0, 1):
+            q = xx * 2 + cc
+            keys, values = kv[cc * 128:cc * 128 + 128, :128], kv[cc * 128:cc * 128 + 128, 128:]
+            ask = qg[q].astype(F32)
+            ask = jnp.concatenate(
+                [jnp.where(first_head, ask, 0.0), jnp.where(first_head, 0.0, ask)], axis=0
+            )
+            exponent = jnp.exp(dot(ask.astype(BF), keys, NT))
+            shares = exponent / jnp.sum(exponent, axis=-1, keepdims=True)
+            mixed = dot(shares.astype(BF), values)
+            context = jnp.where(first_head, mixed[:16], mixed[16:]).astype(BF)
+            part[q] = dot(context, wz[2].reshape(128, width)).astype(BF)
+        for dc in (0, 1):
+            i = dx * 2 + dc
+            cc = lax.rem(c + dc, 2)
+            if i:
+                send(part.at[xx * 2 + cc], pr.at[me8], p_s.at[i], p_r.at[i], at(yh, xx, z, cc))
+
+    attend(0)
+    for k in range(4):
+        far_chunk(k)
+    attend(3)
+    for k in range(4, 8):
+        far_chunk(k)
+    attend(1)
+    attend(2)
+
+    for d in loads[4:10]:
+        d.wait()
     total = dec_ref[...].astype(F32) + part[me8].astype(F32)
     for i, (dx, dc) in enumerate(role[1:], 1):
         q = mod(x - dx, 4) * 2 + lax.rem(c + dc, 2)
@@ -272,12 +338,16 @@
 
     row = lax.broadcasted_iota(jnp.int32, (16, 16), 0)
     col = lax.broadcasted_iota(jnp.int32, (16, 16), 1)
-    id_row, id_col = id_row_ref[...], id_col_ref[...]
+    id_row = jnp.broadcast_to(id_ref[...], (16, 16)).astype(F32)
+    id_col = jnp.sum(jnp.where(row == col, id_row, 0.0), axis=1, keepdims=True)
+    gate = jnp.broadcast_to(gate_ref[...], (16, 16))
+    gate = jnp.sum(jnp.where(row == col, gate, 0.0), axis=1, keepdims=True)
+    id_row = id_row[0:1]
     same = (jnp.broadcast_to(id_row, (16, 16)) == jnp.broadcast_to(id_col, (16, 16))).astype(F32)
     slot_row = jnp.sum(jnp.where(row < col, same, 0.0), axis=0, keepdims=True)
     slot_col = jnp.sum(jnp.where(col < row, same, 0.0), axis=1, keepdims=True)
     number = lax.broadcasted_iota(jnp.int32, (32, 16), 0)
-    chosen = (lax.rem(number, 16) == id_row) & ((number // 16).astype(F32) == slot_row)
+    chosen = (lax.rem(number, 16).astype(F32) == id_row) & ((number // 16).astype(F32) == slot_row)
     picked = dot(chosen.astype(F32).astype(BF), normed)
     ds[:, 0, :] = picked[:16]
     ds[:, 1, :] = picked[16:]
@@ -302,8 +372,6 @@
     for k in (1, 2, 3):
         send(block, block, g_s.at[k], g_r.at[k], at(yh, x, zh * 4 + lax.rem(zl + k, 4), c))
     send(block, block, gs_s.at[0], gs_r.at[0], sibling)
-    for d in loads:
-        d.wait()
     for k in (1, 2, 3):
         block = g.at[mod(zl - k, 4), c]
         arrived(block, g_r.at[k])
@@ -343,9 +411,9 @@
     ds[...] = ret[...].astype(F32)
     slots = jnp.concatenate([ds[:, 0, :], ds[:, 1, :]], axis=0).astype(BF)
     number = lax.broadcasted_iota(jnp.int32, (16, 32), 1)
-    chosen = (lax.rem(number, 16) == id_col) & ((number // 16).astype(F32) == slot_col)
+    chosen = (lax.rem(number, 16).astype(F32) == id_col) & ((number // 16).astype(F32) == slot_col)
     combined = dot(chosen.astype(F32).astype(BF), slots)
-    out_ref[...] = (residual.astype(F32) + gate_ref[...] * combined).astype(BF)
+    out_ref[...] = (residual.astype(F32) + gate * combined).astype(BF)
 
     for d in pending:
         d.wait_send()
@@ -365,6 +433,21 @@
             copy(
                 win.at[s - 1], win.at[s - 1], win_s.at[k - 1], win_r.at[s - 1], sibling
             ).wait_send()
+
+    def sent(ref, sem):
+        copy(ref, ref, sem, sem, sibling).wait_send()
+
+    for k in range(8):
+        for sem in (xr_s, xl_s, x2_s):
+            sent(mem.at[me8, k], sem.at[k])
+        for d in range(4):
+            sent(mem.at[me8, k], sib_s.at[d, k])
+    for r in range(4):
+        for m in range(3):
+            if r < 3 or m < 2:
+                sent(wz.at[m, z], zr_s.at[r, m])
+            if r < 3 or m == 2:
+                sent(wz.at[m, z], zl_s.at[r, m])
 
 
 def per_device(
@@ -376,17 +459,20 @@
     dma = lambda *shape: pltpu.SemaphoreType.DMA(shape)
     vm = lambda *shape: pltpu.VMEM(shape, BF)
     vmem = pl.BlockSpec(memory_space=pltpu.VMEM)
-    smem = pl.BlockSpec(memory_space=pltpu.SMEM)
-    hbm = pl.BlockSpec(memory_space=pl.ANY)
+    hbm = pl.BlockSpec(memory_space=pltpu.HBM)
     scratch = [
+        pltpu.SMEM((1,), jnp.int32), pltpu.SMEM((1,), jnp.int32),
+        vm(width, rows), pltpu.VMEM((1, width), F32), vm(16, width), vm(16, 1024), vm(3, 8, width),
+        pltpu.VMEM((1, width), F32), vm(width, hid), vm(width, hid),
+        pltpu.VMEM((1, 16), jnp.int32), pltpu.VMEM((1, 16), F32),
         vm(8, 16, width), vm(3, 16, width), vm(8, 8, 16, width), vm(2, 3, 8, width),
         vm(3, 8, 16, width), vm(8, 16, 128), vm(8, 16, width), vm(8, 16, width),
         pltpu.VMEM((16, 2, width), F32), vm(16, 2, width), vm(16, 2, width),
         vm(4, 2, 32, width), vm(4, 2, 32, width), vm(4, 32, width), vm(4, 32, width),
-        vm(4, 32, width), vm(16, 2, width), vm(16, 2, width), vm(width, hid), vm(width, hid),
-        dma(2), dma(2), dma(2), dma(8), dma(8), dma(3), dma(3), dma(8), dma(8), dma(1),
+        vm(4, 32, width), vm(16, 2, width), vm(16, 2, width),
+        dma(12), dma(2), dma(2), dma(8), dma(8), dma(3), dma(3), dma(8), dma(8), dma(1),
         dma(8), dma(8), dma(8), dma(8), dma(8), dma(8), dma(4, 8), dma(4, 8),
-        dma(4), dma(4), dma(4), dma(4),
+        dma(4, 3), dma(4, 3), dma(4, 3), dma(4, 3),
         dma(8), dma(8), dma(16), dma(16), dma(4), dma(4), dma(4), dma(4), dma(4), dma(4),
         dma(4), dma(4), dma(16), dma(16),
     ]
@@ -396,17 +482,16 @@
             jax.ShapeDtypeStruct(dec_states.shape[1:], BF),
             jax.ShapeDtypeStruct((8, 16, width), BF),
         ),
-        in_specs=[smem, smem] + [vmem] * 6 + [hbm, hbm] + [vmem] * 3,
+        in_specs=[hbm] * 12,
         out_specs=(vmem, vmem),
         scratch_shapes=scratch,
         compiler_params=pltpu.CompilerParams(
-            collective_id=0, has_side_effects=True, vmem_limit_bytes=50 * 1024 * 1024
+            collective_id=0, has_side_effects=True, vmem_limit_bytes=60 * 1024 * 1024
         ),
     )(
-        patch_start, patch_layer, enc_states[0].reshape(8, 16, width), enc_gain.reshape(1, width),
-        dec_states[0], queries[0], jnp.transpose(attn_weight[0], (0, 2, 1)), ffn_gain,
-        expert_in[0, 0], expert_out[0, 0].T, expert_id[0].reshape(1, 16), expert_id[0],
-        gate.reshape(16, 1),
+        patch_start, patch_layer, enc_states[0].T, enc_gain, dec_states[0], queries[0],
+        jnp.transpose(attn_weight[0], (0, 2, 1)), ffn_gain, expert_in[0, 0], expert_out[0, 0].T,
+        expert_id[0].reshape(1, 16), gate,
     )
     return out[None], memory.reshape(rows, width)
 

time: 142 us -> 126 us (0.89)
  the two profiles are of different devices: /device:TPU:24 before, /device:TPU:1 now
where the time goes in v2:
time: 126 us
  Pallas kernels  121 us (96%)
  local copies, waits for them, and re-layouts  3.58 us (3%)
  between operations  1.93 us (2%)
    pallas_call x1, Pallas kernels, per_device(): pl.pallas_call(kernel, out_shape=(jax.ShapeDtypeStruct(dec_states.shape[1...  121 us
    unnamed x2, local copies, waits for them, and re-layouts  3.58 us

profile of v2, /device:TPU:1, one launch (start us, length us, event | category | flops | bytes accessed | tf_op | source)
XLA Modules:
  0.0 126.2 jit_solution(2614186608127970983)
XLA Ops:
  1.9 120.7 %shard_map.131 = (bf16[16,2080]{1,0:T(8,128)(2,1)}, bf16[8,16,2080]{2,1,0:T(8,128)(2,1)}) custom-call(s32[1]{0:T(128)S(6)} %copy.16.start_hbm, s32[1]{0:T(128)S(6)} %copy.17.layer_hbm, bf16[2080,128]{1,0:T(8,128)(2,1)} %bitcast.18, f32[2080]{0:T(1024)} %enc_gain_hbm.1, bf16[16,2080]{1,0:T(8,128)(2,1)} %bitcast.21, bf16[16,1024]{1,0:T(8,128)(2,1)} %bitcast.22, ...), custom_call_target="tpu_custom_call" | custom-call | tf_op jit(solution)/shard_map/pallas_call | solution.py:479
  122.6 2.1 %copy.14 = bf16[128,2080]{0,1:T(8,128)(2,1)} copy(bf16[128,2080]{1,0:T(8,128)(2,1)} %bitcast.17) | data formatting | bytes 1064960
  124.7 1.5 %copy.18 = bf16[1,16,2080]{2,1,0:T(8,128)(2,1)} copy(bf16[1,16,2080]{2,1,0:T(8,128)(2,1)} %bitcast.20) | data formatting | bytes 133120

commit v3 on v2

--- a/solution.py
+++ b/solution.py
@@ -58,6 +58,8 @@
     up, down = at(yh, x, mod(z + 1, 8), c), at(yh, x, mod(z - 1, 8), c)
     me8 = x * 2 + c
     me16 = yh * 8 + x * 2 + zh
+    side, odd = zl // 2, lax.rem(zl, 2)
+    me32 = me16 * 2 + side
     role = [(dx, dc) for dx in range(4) for dc in range(2)]
 
     def role_of(dx, dc):
@@ -65,14 +67,16 @@
         cc = lax.rem(c + dc, 2)
         return xx, cc
 
-    def expert_of(i):
+    def partner(i, h):
         yy = lax.rem(yh + i // 8, 2)
         xx = mod(x + (i // 2) % 4, 4)
-        if i % 2:
-            zz_h, zz_l = 1 - zh, 3 - zl
-        else:
-            zz_h, zz_l = zh, zl
-        return yy * 8 + xx * 2 + zz_h, at(yy, xx, zz_h * 4 + zz_l, c)
+        zz_h, zz_l = (1 - zh, 1 - odd) if i % 2 else (zh, odd)
+        return yy * 8 + xx * 2 + zz_h, at(yy, xx, zz_h * 4 + zz_l + 2 * h, c)
+
+    def source(i):
+        yy = lax.rem(yh + i // 8, 2)
+        xx = mod(x - (i // 2) % 4, 4)
+        return yy * 8 + xx * 2 + (1 - zh if i % 2 else zh)
 
     pending = []
 
@@ -95,8 +99,6 @@
     peers += [at(yh, *role_of(dx, dc)[:1], z, role_of(dx, dc)[1]) for dx, dc in role[1:]]
     peers += [up, down]
     peers += [at(1 - yh, x, z, cc) for cc in (0, 1)]
-    peers += [at(yh, x, zh * 4 + lax.rem(zl + k, 4), c) for k in (1, 2, 3)]
-    peers += [expert_of(i)[1] for i in range(1, 16)]
     for dev in peers:
         pl.semaphore_signal(barrier, inc=1, device_id=dev, device_id_type=pl.DeviceIdType.MESH)
 
@@ -187,7 +189,6 @@
         scale = lax.rsqrt(jnp.mean(values * values, axis=-1, keepdims=True) + EPS)
         normed = (values * scale * enc_gain_ref[...]).astype(BF)
         mem[me8, k] = normed
-        memory_ref[k] = normed
         block = mem.at[me8, k]
         go(block, block, xr_s.at[k], xr_r.at[k], right)
         go(block, block, xl_s.at[k], xl_r.at[k], left)
@@ -249,7 +250,8 @@
             ring_down(0, m)
 
     first_a = 2 * s
-    first_w, first_z = 3, 5
+    first_w = jnp.where(c == yh, 0, jnp.where(s == 0, 8, 5))
+    first_z = first_w + 2
 
     def tick(t, carry):
         k = t - first_a
@@ -283,7 +285,7 @@
 
         return carry
 
-    lax.fori_loop(0, 17, tick, 0)
+    lax.fori_loop(0, 20, tick, 0)
     from_down(2, 2), from_down(3, 0), from_down(3, 1)
     from_up(2, 0), from_up(2, 1), from_up(3, 2)
     for i, (dx, dc) in enumerate(role[1:], 1):
@@ -324,6 +326,10 @@
     attend(1)
     attend(2)
 
+    row = lax.broadcasted_iota(jnp.int32, (128, 128), 0)
+    col = lax.broadcasted_iota(jnp.int32, (128, 128), 1)
+    turn = (col == row).astype(F32).astype(BF)
+    memory_ref[...] = dot(mem[me8].reshape(128, width), turn, (((0,), (0,)), ((), ()))).astype(BF)
     for d in loads[4:10]:
         d.wait()
     total = dec_ref[...].astype(F32) + part[me8].astype(F32)
@@ -349,69 +355,67 @@
     number = lax.broadcasted_iota(jnp.int32, (32, 16), 0)
     chosen = (lax.rem(number, 16).astype(F32) == id_row) & ((number // 16).astype(F32) == slot_row)
     picked = dot(chosen.astype(F32).astype(BF), normed)
-    ds[:, 0, :] = picked[:16]
-    ds[:, 1, :] = picked[16:]
-    dbuf[...] = ds[...].astype(BF)
-
-    for i in range(1, 16):
-        block, dev = expert_of(i)
-        send(dbuf.at[block], d1.at[me16], d1_s.at[i], d1_r.at[i], dev)
-    d1[me16] = dbuf[me16]
-
-    def back(i):
-        yy = lax.rem(yh + i // 8, 2)
-        xx = mod(x - (i // 2) % 4, 4)
-        return yy * 8 + xx * 2 + (1 - zh if i % 2 else zh)
-
-    for i in range(1, 16):
-        arrived(d1.at[back(i)], d1_r.at[i])
+    ds[0:16, 0, :] = picked[:16]
+    ds[0:16, 1, :] = picked[16:]
+    dbuf[...] = ds[0:16].astype(BF)
+
+    def exchange(block_of, dst, ssem, rsem):
+        for i in range(16):
+            if i == 0:
+                far = lax.rem(zl + 2, 4)
+                send(
+                    block_of(me16, 1 - side), dst.at[me32], ssem.at[0], rsem.at[side],
+                    at(yh, x, zh * 4 + far, c),
+                )
+            else:
+                for h in (0, 1):
+                    e16, dev = partner(i, h)
+                    send(block_of(e16, h), dst.at[me32], ssem.at[i * 2 + h], rsem.at[i * 2 + side], dev)
+
+    def exchanged(dst, rsem):
+        arrived(dst.at[me16 * 2 + (1 - side)], rsem.at[1 - side])
+        for i in range(1, 16):
+            for h in (0, 1):
+                arrived(dst.at[source(i) * 2 + h], rsem.at[i * 2 + h])
+
+    exchange(lambda e16, h: dbuf.at[e16], d1, d1_s, d1_r)
+    d1[me32] = dbuf[me16]
+    exchanged(d1, d1_r)
     ds[...] = d1[...].astype(F32)
-    g[zl, c] = jnp.concatenate([ds[:, 0, :], ds[:, 1, :]], axis=0).astype(BF)
-
-    block = g.at[zl, c]
-    for k in (1, 2, 3):
-        send(block, block, g_s.at[k], g_r.at[k], at(yh, x, zh * 4 + lax.rem(zl + k, 4), c))
+    g[odd, c] = jnp.concatenate([ds[:, 0, :], ds[:, 1, :]], axis=0).astype(BF)
+
+    across = at(yh, x, zh * 4 + zl + 1 - 2 * odd, c)
+    block = g.at[odd, c]
+    send(block, block, g_s.at[0], g_r.at[0], across)
     send(block, block, gs_s.at[0], gs_r.at[0], sibling)
-    for k in (1, 2, 3):
-        block = g.at[mod(zl - k, 4), c]
-        arrived(block, g_r.at[k])
-        send(block, block, gs_s.at[k], gs_r.at[k], sibling)
-    for k in range(4):
-        arrived(g.at[mod(zl - k, 4), 1 - c], gs_r.at[k])
+    block = g.at[1 - odd, c]
+    arrived(block, g_r.at[0])
+    send(block, block, gs_s.at[1], gs_r.at[1], sibling)
+    arrived(g.at[odd, 1 - c], gs_r.at[0])
+    arrived(g.at[1 - odd, 1 - c], gs_r.at[1])
 
     hidden = jnp.maximum(dot(g[...].reshape(256, width), w_in[...]), 0.0).astype(BF)
     y[...] = dot(hidden, w_out[...], NT).astype(BF).reshape(y.shape)
 
-    order = (1, 2, 3, 0)
-    for k in order:
-        to = lax.rem(zl + k, 4)
+    for k in (0, 1):
+        to = lax.rem(odd + 1 + k, 2)
         send(y.at[to, 1 - c], rb.at[to], rb_s.at[k], rb_r.at[k], sibling)
-    for k in order:
-        to = lax.rem(zl + k, 4)
-        arrived(rb.at[to], rb_r.at[k])
-        pair = y[to, c].astype(F32) + rb[to].astype(F32)
-        if k:
-            rt[to] = pair.astype(BF)
-            send(rt.at[to], rz.at[zl], rz_s.at[k], rz_r.at[k], at(yh, x, zh * 4 + to, c))
-        else:
-            total = pair
-    for k in (1, 2, 3):
-        src = mod(zl - k, 4)
-        arrived(rz.at[src], rz_r.at[k])
-        total = total + rz[src].astype(F32)
-    ds[:, 0, :] = total[:16]
-    ds[:, 1, :] = total[16:]
+    arrived(rb.at[1 - odd], rb_r.at[0])
+    rt[...] = (y[1 - odd, c].astype(F32) + rb[1 - odd].astype(F32)).astype(BF)
+    send(rt, rz, rz_s.at[0], rz_r.at[0], across)
+    arrived(rb.at[odd], rb_r.at[1])
+    arrived(rz, rz_r.at[0])
+    total = y[odd, c].astype(F32) + rb[odd].astype(F32) + rz[...].astype(F32)
+    ds[:, 0, :] = total[:32]
+    ds[:, 1, :] = total[32:]
     d2[...] = ds[...].astype(BF)
-    for i in range(1, 16):
-        block, dev = expert_of(i)
-        send(d2.at[block], ret.at[me16], d2_s.at[i], d2_r.at[i], dev)
-    ret[me16] = d2[me16]
-    for i in range(1, 16):
-        arrived(ret.at[back(i)], d2_r.at[i])
+    exchange(lambda e16, h: d2.at[e16 * 2 + h], ret, d2_s, d2_r)
+    ret[me32] = d2[me32]
+    exchanged(ret, d2_r)
     ds[...] = ret[...].astype(F32)
     slots = jnp.concatenate([ds[:, 0, :], ds[:, 1, :]], axis=0).astype(BF)
-    number = lax.broadcasted_iota(jnp.int32, (16, 32), 1)
-    chosen = (lax.rem(number, 16).astype(F32) == id_col) & ((number // 16).astype(F32) == slot_col)
+    number = lax.broadcasted_iota(jnp.int32, (16, 64), 1)
+    chosen = ((lax.rem(number, 32) // 2).astype(F32) == id_col) & ((number // 32).astype(F32) == slot_col)
     combined = dot(chosen.astype(F32).astype(BF), slots)
     out_ref[...] = (residual.astype(F32) + gate * combined).astype(BF)
 
@@ -467,20 +471,20 @@
         pltpu.VMEM((1, 16), jnp.int32), pltpu.VMEM((1, 16), F32),
         vm(8, 16, width), vm(3, 16, width), vm(8, 8, 16, width), vm(2, 3, 8, width),
         vm(3, 8, 16, width), vm(8, 16, 128), vm(8, 16, width), vm(8, 16, width),
-        pltpu.VMEM((16, 2, width), F32), vm(16, 2, width), vm(16, 2, width),
-        vm(4, 2, 32, width), vm(4, 2, 32, width), vm(4, 32, width), vm(4, 32, width),
-        vm(4, 32, width), vm(16, 2, width), vm(16, 2, width),
+        pltpu.VMEM((32, 2, width), F32), vm(16, 2, width), vm(32, 2, width),
+        vm(2, 2, 64, width), vm(2, 2, 64, width), vm(2, 64, width), vm(64, width), vm(64, width),
+        vm(32, 2, width), vm(32, 2, width),
         dma(12), dma(2), dma(2), dma(8), dma(8), dma(3), dma(3), dma(8), dma(8), dma(1),
         dma(8), dma(8), dma(8), dma(8), dma(8), dma(8), dma(4, 8), dma(4, 8),
         dma(4, 3), dma(4, 3), dma(4, 3), dma(4, 3),
-        dma(8), dma(8), dma(16), dma(16), dma(4), dma(4), dma(4), dma(4), dma(4), dma(4),
-        dma(4), dma(4), dma(16), dma(16),
+        dma(8), dma(8), dma(32), dma(32), dma(1), dma(1), dma(2), dma(2), dma(2), dma(2),
+        dma(1), dma(1), dma(32), dma(32),
     ]
     out, memory = pl.pallas_call(
         kernel,
         out_shape=(
             jax.ShapeDtypeStruct(dec_states.shape[1:], BF),
-            jax.ShapeDtypeStruct((8, 16, width), BF),
+            jax.ShapeDtypeStruct((width, rows), BF),
         ),
         in_specs=[hbm] * 12,
         out_specs=(vmem, vmem),
@@ -493,7 +497,7 @@
         jnp.transpose(attn_weight[0], (0, 2, 1)), ffn_gain, expert_in[0, 0], expert_out[0, 0].T,
         expert_id[0].reshape(1, 16), gate,
     )
-    return out[None], memory.reshape(rows, width)
+    return out[None], memory.T
 
 
 def solution(mesh):

time: 126 us -> 119 us (0.944)
  Pallas kernels: 121 us -> 113 us
    pallas_call x1, Pallas kernels: 121 us -> 113 us  [per_device(): pl.pallas_call(kernel, out_shape=(jax.ShapeDtypeStruct(dec_states.shape[1...]
where the time goes in v3:
time: 119 us; the launch traced here: 118 us
  Pallas kernels  113 us (95%)
  local copies, waits for them, and re-layouts  3.39 us (3%)
  between operations  1.93 us (2%)
    pallas_call x1, Pallas kernels, per_device(): pl.pallas_call(kernel, out_shape=(jax.ShapeDtypeStruct(dec_states.shape[1...  113 us
    unnamed x2, local copies, waits for them, and re-layouts  3.39 us

profile of v3, /device:TPU:1, one launch (start us, length us, event | category | flops | bytes accessed | tf_op | source)
XLA Modules:
  0.0 118.3 jit_solution(17516302408058577117)
XLA Ops:
  1.9 113.0 %shard_map.131 = (bf16[16,2080]{1,0:T(8,128)(2,1)}, bf16[2080,128]{1,0:T(8,128)(2,1)}) custom-call(s32[1]{0:T(128)S(6)} %copy.16.start_hbm, s32[1]{0:T(128)S(6)} %copy.17.layer_hbm, bf16[2080,128]{1,0:T(8,128)(2,1)} %bitcast.17, f32[2080]{0:T(1024)} %enc_gain_hbm.1, bf16[16,2080]{1,0:T(8,128)(2,1)} %bitcast.21, bf16[16,1024]{1,0:T(8,128)(2,1)} %bitcast.22, ...), custom_call_target="tpu_custom_call" | custom-call | tf_op jit(solution)/shard_map/pallas_call | solution.py:483
  115.0 1.5 %copy.18 = bf16[1,16,2080]{2,1,0:T(8,128)(2,1)} copy(bf16[1,16,2080]{2,1,0:T(8,128)(2,1)} %bitcast.20) | data formatting | bytes 133120
  116.5 1.9 %copy.19 = bf16[128,2080]{0,1:T(8,128)(2,1)} copy(bf16[128,2080]{0,1:T(8,128)(2,1)} %bitcast.18) | data formatting | bytes 1064960

commit v4 on v3

--- a/solution.py
+++ b/solution.py
@@ -59,7 +59,7 @@
     me8 = x * 2 + c
     me16 = yh * 8 + x * 2 + zh
     side, odd = zl // 2, lax.rem(zl, 2)
-    me32 = me16 * 2 + side
+    me_src = (x * 2 + zh) * 2 + side
     role = [(dx, dc) for dx in range(4) for dc in range(2)]
 
     def role_of(dx, dc):
@@ -74,9 +74,8 @@
         return yy * 8 + xx * 2 + zz_h, at(yy, xx, zz_h * 4 + zz_l + 2 * h, c)
 
     def source(i):
-        yy = lax.rem(yh + i // 8, 2)
         xx = mod(x - (i // 2) % 4, 4)
-        return yy * 8 + xx * 2 + (1 - zh if i % 2 else zh)
+        return (xx * 2 + (1 - zh if i % 2 else zh)) * 2
 
     pending = []
 
@@ -118,9 +117,9 @@
 
     @pl.when(s > 0)
     def _():
-        row = lax.broadcasted_iota(jnp.int32, (16, 128), 0)
-        col = lax.broadcasted_iota(jnp.int32, (16, 128), 1)
-        pick = ((col == row + start) & (row < PATCH)).astype(F32).astype(BF)
+        row = lax.broadcasted_iota(jnp.int32, (PATCH, 128), 0)
+        col = lax.broadcasted_iota(jnp.int32, (PATCH, 128), 1)
+        pick = (col == row + start).astype(F32).astype(BF)
         win[s - 1] = dot(pick, enc_ref[...], NT).astype(BF)
 
     pl.semaphore_wait(barrier, len(peers))
@@ -179,9 +178,9 @@
                 arrived(win.at[i], win_r.at[i])
 
         first = k * CHUNK - start
-        row = lax.broadcasted_iota(jnp.int32, (CHUNK, 16), 0) + first
-        slot = lax.broadcasted_iota(jnp.int32, (CHUNK, 16), 1)
-        pick = ((row == slot) & (slot < PATCH)).astype(F32).astype(BF)
+        row = lax.broadcasted_iota(jnp.int32, (CHUNK, PATCH), 0) + first
+        slot = lax.broadcasted_iota(jnp.int32, (CHUNK, PATCH), 1)
+        pick = (row == slot).astype(F32).astype(BF)
         window = jnp.where(layer == 1, win[0], jnp.where(layer == 2, win[1], win[2]))
         fresh = dot(pick, window)
         at_row = lax.broadcasted_iota(jnp.int32, fresh.shape, 0) + first
@@ -251,7 +250,7 @@
 
     first_a = 2 * s
     first_w = jnp.where(c == yh, 0, jnp.where(s == 0, 8, 5))
-    first_z = first_w + 2
+    first_z = first_w + 1
 
     def tick(t, carry):
         k = t - first_a
@@ -270,22 +269,23 @@
         def _():
             neighbour_chunk(kb)
 
-        j = t - first_z
-        r, m = j // 3, lax.rem(j, 3)
-
-        @pl.when((j >= 0) & (j < 8))
-        def _():
-            from_down(r, m)
-            ring_up(r + 1, m)
-
-        @pl.when((j >= 0) & ((j < 6) | (j == 8)))
-        def _():
-            from_up(r, m)
-            ring_down(r + 1, m)
+        for half in (0, 1):
+            j = (t - first_z) * 2 + half
+            r, m = j // 3, lax.rem(j, 3)
+
+            @pl.when((j >= 0) & (j < 8))
+            def _(r=r, m=m):
+                from_down(r, m)
+                ring_up(r + 1, m)
+
+            @pl.when((j >= 0) & ((j < 6) | (j == 8)))
+            def _(r=r, m=m):
+                from_up(r, m)
+                ring_down(r + 1, m)
 
         return carry
 
-    lax.fori_loop(0, 20, tick, 0)
+    lax.fori_loop(0, 18, tick, 0)
     from_down(2, 2), from_down(3, 0), from_down(3, 1)
     from_up(2, 0), from_up(2, 1), from_up(3, 2)
     for i, (dx, dc) in enumerate(role[1:], 1):
@@ -355,68 +355,91 @@
     number = lax.broadcasted_iota(jnp.int32, (32, 16), 0)
     chosen = (lax.rem(number, 16).astype(F32) == id_row) & ((number // 16).astype(F32) == slot_row)
     picked = dot(chosen.astype(F32).astype(BF), normed)
-    ds[0:16, 0, :] = picked[:16]
-    ds[0:16, 1, :] = picked[16:]
-    dbuf[...] = ds[0:16].astype(BF)
-
-    def exchange(block_of, dst, ssem, rsem):
-        for i in range(16):
+    ds[:, 0, :] = picked[:16]
+    ds[:, 1, :] = picked[16:]
+    dbuf[...] = ds[...].astype(BF)
+
+    far_first = sorted(range(16), key=lambda i: (i // 8, min(i // 2 % 4, 4 - i // 2 % 4) + 2 * (i % 2)))[::-1]
+
+    def exchange(group, block_of, dst, ssem, rsem):
+        for i in far_first:
+            if i // 8 != group:
+                continue
             if i == 0:
-                far = lax.rem(zl + 2, 4)
                 send(
-                    block_of(me16, 1 - side), dst.at[me32], ssem.at[0], rsem.at[side],
-                    at(yh, x, zh * 4 + far, c),
+                    block_of(me16, 1 - side), dst.at[0, me_src], ssem.at[0], rsem.at[side],
+                    at(yh, x, zh * 4 + lax.rem(zl + 2, 4), c),
                 )
             else:
                 for h in (0, 1):
                     e16, dev = partner(i, h)
-                    send(block_of(e16, h), dst.at[me32], ssem.at[i * 2 + h], rsem.at[i * 2 + side], dev)
-
-    def exchanged(dst, rsem):
-        arrived(dst.at[me16 * 2 + (1 - side)], rsem.at[1 - side])
-        for i in range(1, 16):
-            for h in (0, 1):
-                arrived(dst.at[source(i) * 2 + h], rsem.at[i * 2 + h])
-
-    exchange(lambda e16, h: dbuf.at[e16], d1, d1_s, d1_r)
-    d1[me32] = dbuf[me16]
-    exchanged(d1, d1_r)
-    ds[...] = d1[...].astype(F32)
-    g[odd, c] = jnp.concatenate([ds[:, 0, :], ds[:, 1, :]], axis=0).astype(BF)
+                    send(
+                        block_of(e16, h), dst.at[group, me_src],
+                        ssem.at[i * 2 + h], rsem.at[i * 2 + side], dev,
+                    )
+
+    def exchanged(group, dst, rsem):
+        for i in range(group * 8, group * 8 + 8):
+            if i == 0:
+                arrived(dst.at[0, (x * 2 + zh) * 2 + (1 - side)], rsem.at[1 - side])
+            else:
+                for h in (0, 1):
+                    arrived(dst.at[group, source(i) + h], rsem.at[i * 2 + h])
 
     across = at(yh, x, zh * 4 + zl + 1 - 2 * odd, c)
-    block = g.at[odd, c]
-    send(block, block, g_s.at[0], g_r.at[0], across)
-    send(block, block, gs_s.at[0], gs_r.at[0], sibling)
-    block = g.at[1 - odd, c]
-    arrived(block, g_r.at[0])
-    send(block, block, gs_s.at[1], gs_r.at[1], sibling)
-    arrived(g.at[odd, 1 - c], gs_r.at[0])
-    arrived(g.at[1 - odd, 1 - c], gs_r.at[1])
-
-    hidden = jnp.maximum(dot(g[...].reshape(256, width), w_in[...]), 0.0).astype(BF)
-    y[...] = dot(hidden, w_out[...], NT).astype(BF).reshape(y.shape)
-
-    for k in (0, 1):
-        to = lax.rem(odd + 1 + k, 2)
-        send(y.at[to, 1 - c], rb.at[to], rb_s.at[k], rb_r.at[k], sibling)
-    arrived(rb.at[1 - odd], rb_r.at[0])
-    rt[...] = (y[1 - odd, c].astype(F32) + rb[1 - odd].astype(F32)).astype(BF)
-    send(rt, rz, rz_s.at[0], rz_r.at[0], across)
-    arrived(rb.at[odd], rb_r.at[1])
-    arrived(rz, rz_r.at[0])
-    total = y[odd, c].astype(F32) + rb[odd].astype(F32) + rz[...].astype(F32)
-    ds[:, 0, :] = total[:32]
-    ds[:, 1, :] = total[32:]
-    d2[...] = ds[...].astype(BF)
-    exchange(lambda e16, h: d2.at[e16 * 2 + h], ret, d2_s, d2_r)
-    ret[me32] = d2[me32]
-    exchanged(ret, d2_r)
-    ds[...] = ret[...].astype(F32)
-    slots = jnp.concatenate([ds[:, 0, :], ds[:, 1, :]], axis=0).astype(BF)
-    number = lax.broadcasted_iota(jnp.int32, (16, 64), 1)
-    chosen = ((lax.rem(number, 32) // 2).astype(F32) == id_col) & ((number // 32).astype(F32) == slot_col)
-    combined = dot(chosen.astype(F32).astype(BF), slots)
+
+    for group in (1, 0):
+        exchange(group, lambda e16, h: dbuf.at[e16], d1, d1_s, d1_r)
+    d1[0, me_src] = dbuf[me16]
+
+    def share(group):
+        exchanged(group, d1, d1_r)
+        ds[...] = d1[group].astype(F32)
+        g[group, odd, c] = jnp.concatenate([ds[:, 0, :], ds[:, 1, :]], axis=0).astype(BF)
+        block = g.at[group, odd, c]
+        send(block, block, g_s.at[group], g_r.at[group], across)
+        send(block, block, gs_s.at[group, 0], gs_r.at[group, 0], sibling)
+
+    def shared(group):
+        block = g.at[group, 1 - odd, c]
+        arrived(block, g_r.at[group])
+        send(block, block, gs_s.at[group, 1], gs_r.at[group, 1], sibling)
+
+    def work(group):
+        for k in (0, 1):
+            arrived(g.at[group, odd if k == 0 else 1 - odd, 1 - c], gs_r.at[group, k])
+        hidden = jnp.maximum(dot(g[group].reshape(128, width), w_in[...]), 0.0).astype(BF)
+        y[group] = dot(hidden, w_out[...], NT).astype(BF).reshape(2, 2, 32, width)
+        for k in (0, 1):
+            to = lax.rem(odd + 1 + k, 2)
+            send(y.at[group, to, 1 - c], rb.at[group, to], rb_s.at[group, k], rb_r.at[group, k], sibling)
+
+    def pair_sum(group):
+        arrived(rb.at[group, 1 - odd], rb_r.at[group, 0])
+        rt[group] = (y[group, 1 - odd, c].astype(F32) + rb[group, 1 - odd].astype(F32)).astype(BF)
+        send(rt.at[group], rz.at[group], rz_s.at[group], rz_r.at[group], across)
+
+    def give_back(group):
+        arrived(rb.at[group, odd], rb_r.at[group, 1])
+        arrived(rz.at[group], rz_r.at[group])
+        total = y[group, odd, c].astype(F32) + rb[group, odd].astype(F32) + rz[group].astype(F32)
+        ds[:, 0, :] = total[:16]
+        ds[:, 1, :] = total[16:]
+        d2[group] = ds[...].astype(BF)
+        exchange(group, lambda e16, h: d2.at[group, lax.rem(e16, 8) * 2 + h], ret, d2_s, d2_r)
+
+    share(0), shared(0), share(1), work(0), shared(1), pair_sum(0)
+    work(1), pair_sum(1), give_back(1), give_back(0)
+    ret[0, me_src] = d2[0, me_src]
+    combined = jnp.zeros((16, width), F32)
+    number = lax.broadcasted_iota(jnp.int32, (16, 32), 1)
+    for group in (0, 1):
+        exchanged(group, ret, d2_r)
+        ds[...] = ret[group].astype(F32)
+        slots = jnp.concatenate([ds[:, 0, :], ds[:, 1, :]], axis=0).astype(BF)
+        expert = lax.rem(number, 16) // 2 + 8 * lax.rem(yh + group, 2)
+        chosen = (expert.astype(F32) == id_col) & ((number // 16).astype(F32) == slot_col)
+        combined = combined + dot(chosen.astype(F32).astype(BF), slots)
     out_ref[...] = (residual.astype(F32) + gate * combined).astype(BF)
 
     for d in pending:
@@ -469,16 +492,16 @@
         vm(width, rows), pltpu.VMEM((1, width), F32), vm(16, width), vm(16, 1024), vm(3, 8, width),
         pltpu.VMEM((1, width), F32), vm(width, hid), vm(width, hid),
         pltpu.VMEM((1, 16), jnp.int32), pltpu.VMEM((1, 16), F32),
-        vm(8, 16, width), vm(3, 16, width), vm(8, 8, 16, width), vm(2, 3, 8, width),
+        vm(8, 16, width), vm(3, PATCH, width), vm(8, 8, 16, width), vm(2, 3, 8, width),
         vm(3, 8, 16, width), vm(8, 16, 128), vm(8, 16, width), vm(8, 16, width),
-        pltpu.VMEM((32, 2, width), F32), vm(16, 2, width), vm(32, 2, width),
-        vm(2, 2, 64, width), vm(2, 2, 64, width), vm(2, 64, width), vm(64, width), vm(64, width),
-        vm(32, 2, width), vm(32, 2, width),
+        pltpu.VMEM((16, 2, width), F32), vm(16, 2, width), vm(2, 16, 2, width),
+        vm(2, 2, 2, 32, width), vm(2, 2, 2, 32, width), vm(2, 2, 32, width), vm(2, 32, width),
+        vm(2, 32, width), vm(2, 16, 2, width), vm(2, 16, 2, width),
         dma(12), dma(2), dma(2), dma(8), dma(8), dma(3), dma(3), dma(8), dma(8), dma(1),
         dma(8), dma(8), dma(8), dma(8), dma(8), dma(8), dma(4, 8), dma(4, 8),
         dma(4, 3), dma(4, 3), dma(4, 3), dma(4, 3),
-        dma(8), dma(8), dma(32), dma(32), dma(1), dma(1), dma(2), dma(2), dma(2), dma(2),
-        dma(1), dma(1), dma(32), dma(32),
+        dma(8), dma(8), dma(32), dma(32), dma(2), dma(2), dma(2, 2), dma(2, 2), dma(2, 2), dma(2, 2),
+        dma(2), dma(2), dma(32), dma(32),
     ]
     out, memory = pl.pallas_call(
         kernel,

time: 119 us -> 109 us (0.916)
  Pallas kernels: 113 us -> 104 us
    pallas_call x1, Pallas kernels: 113 us -> 104 us  [per_device(): pl.pallas_call(kernel, out_shape=(jax.ShapeDtypeStruct(dec_states.shape[1...]
where the time goes in v4:
time: 109 us
  Pallas kernels  104 us (95%)
  local copies, waits for them, and re-layouts  3.39 us (3%)
  between operations  1.93 us (2%)
    pallas_call x1, Pallas kernels, per_device(): pl.pallas_call(kernel, out_shape=(jax.ShapeDtypeStruct(dec_states.shape[1...  104 us
    unnamed x2, local copies, waits for them, and re-layouts  3.39 us

profile of v4, /device:TPU:1, one launch (start us, length us, event | category | flops | bytes accessed | tf_op | source)
XLA Modules:
  0.0 109.1 jit_solution(216596292080540051)
XLA Ops:
  1.9 103.8 %shard_map.131 = (bf16[16,2080]{1,0:T(8,128)(2,1)}, bf16[2080,128]{1,0:T(8,128)(2,1)}) custom-call(s32[1]{0:T(128)S(6)} %copy.16.start_hbm, s32[1]{0:T(128)S(6)} %copy.17.layer_hbm, bf16[2080,128]{1,0:T(8,128)(2,1)} %bitcast.17, f32[2080]{0:T(1024)} %enc_gain_hbm.1, bf16[16,2080]{1,0:T(8,128)(2,1)} %bitcast.21, bf16[16,1024]{1,0:T(8,128)(2,1)} %bitcast.22, ...), custom_call_target="tpu_custom_call" | custom-call | tf_op jit(solution)/shard_map/pallas_call | solution.py:506
  105.7 1.5 %copy.18 = bf16[1,16,2080]{2,1,0:T(8,128)(2,1)} copy(bf16[1,16,2080]{2,1,0:T(8,128)(2,1)} %bitcast.20) | data formatting | bytes 133120
  107.2 1.9 %copy.19 = bf16[128,2080]{0,1:T(8,128)(2,1)} copy(bf16[128,2080]{0,1:T(8,128)(2,1)} %bitcast.18) | data formatting | bytes 1064960

commit v5 on v4

--- a/solution.py
+++ b/solution.py
@@ -263,7 +263,7 @@
         def _():
             own_weights()
 
-        kb = k - 3
+        kb = k - 4
 
         @pl.when((kb >= 0) & (kb < 8))
         def _():
@@ -285,7 +285,7 @@
 
         return carry
 
-    lax.fori_loop(0, 18, tick, 0)
+    lax.fori_loop(0, 19, tick, 0)
     from_down(2, 2), from_down(3, 0), from_down(3, 1)
     from_up(2, 0), from_up(2, 1), from_up(3, 2)
     for i, (dx, dc) in enumerate(role[1:], 1):

time: 109 us -> 108 us (level)
  the two profiles are of different devices: /device:TPU:1 before, /device:TPU:24 now
where the time goes in v5:
time: 108 us
  Pallas kernels  103 us (95%)
  local copies, waits for them, and re-layouts  3.39 us (3%)
  between operations  1.93 us (2%)
    pallas_call x1, Pallas kernels, per_device(): pl.pallas_call(kernel, out_shape=(jax.ShapeDtypeStruct(dec_states.shape[1...  103 us
    unnamed x2, local copies, waits for them, and re-layouts  3.39 us

profile of v5, /device:TPU:24, one launch (start us, length us, event | category | flops | bytes accessed | tf_op | source)
XLA Modules:
  0.0 108.1 jit_solution(761442505475326779)
XLA Ops:
  1.9 102.8 %shard_map.131 = (bf16[16,2080]{1,0:T(8,128)(2,1)}, bf16[2080,128]{1,0:T(8,128)(2,1)}) custom-call(s32[1]{0:T(128)S(6)} %copy.16.start_hbm, s32[1]{0:T(128)S(6)} %copy.17.layer_hbm, bf16[2080,128]{1,0:T(8,128)(2,1)} %bitcast.17, f32[2080]{0:T(1024)} %enc_gain_hbm.1, bf16[16,2080]{1,0:T(8,128)(2,1)} %bitcast.21, bf16[16,1024]{1,0:T(8,128)(2,1)} %bitcast.22, ...), custom_call_target="tpu_custom_call" | custom-call | tf_op jit(solution)/shard_map/pallas_call | solution.py:506
  104.7 1.5 %copy.18 = bf16[1,16,2080]{2,1,0:T(8,128)(2,1)} copy(bf16[1,16,2080]{2,1,0:T(8,128)(2,1)} %bitcast.20) | data formatting | bytes 133120
  106.2 1.9 %copy.19 = bf16[128,2080]{0,1:T(8,128)(2,1)} copy(bf16[128,2080]{0,1:T(8,128)(2,1)} %bitcast.18) | data formatting | bytes 1064960
